TPU v7x, 32 devices: a whole 2x2x4 slice. The times are simulated.
32 devices in a mesh: rows: 16 (over z, y, x), rep: 2 (over core).
Axes of the slice: x: 2, y: 2, z: 4, core: 2. Of those that a mesh axis runs over, the one named last changes fastest.
Arguments:
- entity_table: bfloat16 [98304, 256], P('rows'), may hold values from -3 to 3
- relation_ops: bfloat16 [8, 256, 256], replicated, may hold values from -0.375 to 0.375
- need_rows: int32 [16, 2, 16, 8], P('rows', 'rep'), may hold values from 0 to 6143
- send_offsets: int32 [16, 2, 17], P('rows', 'rep'), may hold values from 0 to 128, as said below
- source_ids: int32 [16, 2, 2, 1024], P('rows', 'rep'), may hold values from 0 to 127, as said below
- target_ids: int32 [16, 2, 2, 1024], P('rows', 'rep'), may hold values from 0 to 127, as said below
- negative_ids: int32 [16, 2, 2, 1024], P('rows', 'rep'), may hold values from 0 to 127, as said below
- relation_ids: int32 [16, 2, 2], P('rows', 'rep'), may hold values from 0 to 7
Outputs:
- entity_grad: bfloat16 [98304, 256], P(('rows', 'rep'))
- relation_grad: float32 [8, 256, 256], replicated
Inputs may be any that keep to these rules, and one draw needn't show every extreme that they name: `send_offsets`: along the last dimension the offsets start at 0 and rise by 2 to 8 from owner to owner; there is one owner, the same for every device, from which every device requests exactly 8 rows (rise of 8), and there is one device that requests 8 rows from every owner. `source_ids`: each id is below the device's last entry of send_offsets; on every device some id is 0 and some id is that last entry minus 1. `target_ids`: each id is below the device's last entry of send_offsets; on every device some id is 0 and some id is that last entry minus 1. `negative_ids`: each id is below the device's last entry of send_offsets; on every device some id is 0 and some id is that last entry minus 1. `need_rows`: entries past an owner's count of requested rows are not referenced.
All inputs are finite; a program needn't handle non-finite values.
Results may differ from a plain program's by a relative error of at most 0.0065.
Values may be sent and summed in bfloat16 or wider, within the bound.
A program may use at most 64 MiB of HBM per device.

v0:
```python
import jax
import jax.numpy as jnp
from jax import lax
from jax.sharding import PartitionSpec as P


def locate(edge_ids, offsets, capacity):
    upper_bound = offsets[1:]
    lower_bound = offsets[:-1]
    owner_index = jnp.sum((edge_ids[..., None] >= upper_bound).astype(jnp.int32), axis=-1)
    start_slot = jnp.max(jnp.where(edge_ids[..., None] >= lower_bound, lower_bound, 0), axis=-1)
    return owner_index * capacity + edge_ids - start_slot


def block_terms(source, target, negative, operator, weight_neg):
    query = jnp.dot(source, operator, preferred_element_type=jnp.float32).astype(jnp.bfloat16)
    positive = jnp.einsum("bd,bd->b", query, target, preferred_element_type=jnp.float32)
    scores = jnp.einsum("bd,nd->bn", query, negative, preferred_element_type=jnp.float32)
    slope = -jax.nn.sigmoid(-positive)
    neg_weight = (jax.nn.sigmoid(scores) * weight_neg).astype(jnp.bfloat16)
    query_grad = slope[:, None] * target.astype(jnp.float32) + jnp.dot(
        neg_weight, negative, preferred_element_type=jnp.float32
    )
    query_grad = query_grad.astype(jnp.bfloat16)
    target_grad = slope[:, None] * query.astype(jnp.float32)
    negative_grad = jnp.einsum("bn,bd->nd", neg_weight, query, preferred_element_type=jnp.float32)
    source_grad = jnp.einsum("bd,ed->be", query_grad, operator, preferred_element_type=jnp.float32)
    operator_grad = jnp.einsum("be,bd->ed", source, query_grad, preferred_element_type=jnp.float32)
    return (source_grad, target_grad, negative_grad, operator_grad)


def shards(
    entity_table,
    relation_ops,
    need_rows,
    send_offsets,
    source_ids,
    target_ids,
    negative_ids,
    relation_ids,
):
    requests = need_rows[0, 0]
    owner_count, capacity = requests.shape
    row_width = entity_table.shape[1]
    received = lax.all_to_all(requests, "rows", split_axis=0, concat_axis=0, tiled=True)
    serve_picked = jnp.take(entity_table, received, axis=0)
    returned = lax.all_to_all(serve_picked, "rows", split_axis=0, concat_axis=0, tiled=True)
    fetched = returned
    slot_count = owner_count * capacity
    slots = fetched.reshape(slot_count, row_width)
    offsets = send_offsets[0, 0]
    source_slot = locate(source_ids[0, 0], offsets, capacity)
    target_slot = locate(target_ids[0, 0], offsets, capacity)
    negative_slot = locate(negative_ids[0, 0], offsets, capacity)
    relations = relation_ids[0, 0]
    edge_count = source_ids.shape[-1]
    weight_neg = negative_ids.shape[-1] ** (-0.5)
    slot_lane = jnp.arange(slot_count, dtype=jnp.int32)
    relation_lane = jnp.arange(relation_ops.shape[0], dtype=jnp.int32)
    slot_grad = jnp.zeros((slot_count, row_width), jnp.float32)
    operator_acc = jnp.zeros(relation_ops.shape, jnp.float32)
    for block_index in range(relations.shape[0]):
        joined_slot = jnp.concatenate(
            [source_slot[block_index], target_slot[block_index], negative_slot[block_index]], axis=0
        )
        picker = (joined_slot[:, None] == slot_lane[None, :]).astype(jnp.bfloat16)
        picked = jnp.dot(picker, slots, preferred_element_type=jnp.float32).astype(jnp.bfloat16)
        source = picked[:edge_count]
        target = picked[edge_count : 2 * edge_count]
        negative = picked[2 * edge_count :]
        operator = lax.dynamic_index_in_dim(relation_ops, relations[block_index], 0, keepdims=False)
        source_grad, target_grad, negative_grad, operator_grad = block_terms(
            source, target, negative, operator, weight_neg
        )
        joined_grad = jnp.concatenate([source_grad, target_grad, negative_grad], axis=0)
        upper_part = joined_grad.astype(jnp.bfloat16)
        lower_part = (joined_grad - upper_part.astype(jnp.float32)).astype(jnp.bfloat16)
        slot_grad = slot_grad + jnp.einsum(
            "rs,rd->sd", picker, upper_part, preferred_element_type=jnp.float32
        )
        slot_grad = slot_grad + jnp.einsum(
            "rs,rd->sd", picker, lower_part, preferred_element_type=jnp.float32
        )
        chosen = (relation_lane == relations[block_index]).astype(jnp.float32)
        operator_acc = operator_acc + chosen[:, None, None] * operator_grad[None, :, :]
    operator_total = lax.psum(operator_acc, ("rows", "rep"))
    devices = lax.axis_size("rows") * lax.axis_size("rep")
    relation_grad = (
        operator_total
        * (relation_ops.shape[0] / (edge_count * relations.shape[0] * devices)) ** 0.5
    )
    returned = lax.all_to_all(
        slot_grad.reshape(owner_count, capacity, row_width),
        "rows",
        split_axis=0,
        concat_axis=0,
        tiled=True,
    )
    flat_index = received.reshape(-1)
    flat_grad = returned.reshape(-1, row_width)
    owner_slab = (
        jnp.zeros((entity_table.shape[0], row_width), jnp.float32).at[flat_index].add(flat_grad)
    )
    entity_grad = lax.psum_scatter(owner_slab, "rep", scatter_dimension=0, tiled=True)
    return (entity_grad.astype(jnp.bfloat16), relation_grad)


def solution(mesh):
    return jax.shard_map(
        shards,
        mesh=mesh,
        in_specs=(
            P("rows", None),
            P(),
            P("rows", "rep", None, None),
            P("rows", "rep", None),
            P("rows", "rep", None, None),
            P("rows", "rep", None, None),
            P("rows", "rep", None, None),
            P("rows", "rep", None),
        ),
        out_specs=(P(("rows", "rep"), None), P()),
        check_vma=False,
    )
```

profile of v0, /device:TPU:0, one launch (start us, length us, event | category | flops | bytes accessed | tf_op | source)
XLA Modules:
  0.0 207.0 jit_solution(2638052348424822502)
XLA Ops:
  8.0 1.5 copy.21
  9.5 8.3 %all-to-all-start = ((s32[16,1,8]{2,1,0:T(1,128)}), s32[16,1,8]{2,1,0:T(1,128)S(1)}, u32[]{:S(2)}, u32[]{:S(2)}) async-start(s32[16,1,8]{2,1,0:T(1,128)} %copy.21), calls=%async_computation | async-start | bytes 16384 | tf_op jit(solution)/shard_map/all_to_all | solution.py:45
  17.8 0.8 slice_bitcast_fusion
  18.6 1.0 convert_reduce_fusion
  21.2 1.4 fusion.69
  22.6 2.5 %all-to-all-done = s32[16,1,8]{2,1,0:T(1,128)S(1)} async-done(((s32[16,1,8]{2,1,0:T(1,128)}), s32[16,1,8]{2,1,0:T(1,128)S(1)}, u32[]{:S(2)}, u32[]{:S(2)}) %all-to-all-start) | async-done | bytes 544 | tf_op jit(solution)/shard_map/all_to_all | solution.py:45
  25.4 0.8 gather_fusion
  27.0 4.4 %all-to-all-start.1 = ((bf16[16,8,256]{2,1,0:T(8,128)(2,1)}), bf16[16,8,256]{2,1,0:T(8,128)(2,1)S(1)}, u32[]{:S(2)}, u32[]{:S(2)}) async-start(bf16[16,8,256]{2,1,0:T(8,128)(2,1)} %bitcast_select_fusion), calls=%async_computation.1 | async-start | bytes 131072 | tf_op jit(solution)/shard_map/all_to_all | solution.py:47
  31.4 1.3 compare_convert_fusion
  36.8 2.1 %all-to-all-done.1 = bf16[16,8,256]{2,1,0:T(8,128)(2,1)S(1)} async-done(((bf16[16,8,256]{2,1,0:T(8,128)(2,1)}), bf16[16,8,256]{2,1,0:T(8,128)(2,1)S(1)}, u32[]{:S(2)}, u32[]{:S(2)}) %all-to-all-start.1) | async-done | bytes 65568 | tf_op jit(solution)/shard_map/all_to_all | solution.py:47
  38.9 1.6 convolution_convert_fusion.1
  40.6 1.3 fusion.26
  41.9 1.3 multiply_convert_fusion.1
  43.2 1.3 convert_multiply_fusion.2
  45.6 2.2 %fusion.48 = f32[1024,256]{1,0:T(8,128)} fusion(bf16[1024,256]{1,0:T(8,128)(2,1)S(1)} %fusion.12, bf16[8,256,256]{2,1,0:T(8,128)(2,1)} %param.9, s32[]{:T(128)S(6)} %select_n.54), kind=kOutput, calls=%fused_computation.60 | convolution fusion | flops 134217728 | bytes 1703940 | tf_op jit(solution)/shard_map/bd,ed->be/dot_general | solution.py:27
  47.9 1.8 convolution_convert_fusion
  49.7 1.3 fusion.27
  51.0 1.3 multiply_convert_fusion
  53.2 0.7 fusion.71
  54.3 1.2 fusion.45
  55.6 1.1 fusion.4
  56.6 1.1 fusion.5
  57.7 1.7 multiply_add_fusion
  59.5 2.6 %fusion.70 = f32[1024,256]{1,0:T(8,128)S(1)} fusion(bf16[1024,1024]{1,0:T(8,128)(2,1)} %copy-done.4, bf16[1024,256]{1,0:T(8,128)(2,1)} %copy-done.3), kind=kOutput, calls=%fused_computation.105 | convolution fusion | flops 536870912 | bytes 3670016 | tf_op jit(solution)/shard_map/bn,bd->nd/dot_general | solution.py:26
  62.1 1.1 fusion.6
  63.1 1.7 fusion.23
  64.9 4.8 %all-to-all-start.2 = ((f32[16,8,256]{2,1,0:T(8,128)}), f32[16,8,256]{2,1,0:T(8,128)S(1)}, u32[]{:S(2)}, u32[]{:S(2)}) async-start(f32[16,8,256]{2,1,0:T(8,128)} %fusion.23), calls=%async_computation.2 | async-start | bytes 262144 | tf_op jit(solution)/shard_map/all_to_all | solution.py:92
  71.0 6.8 %all-to-all-done.2 = f32[16,8,256]{2,1,0:T(8,128)S(1)} async-done(((f32[16,8,256]{2,1,0:T(8,128)}), f32[16,8,256]{2,1,0:T(8,128)S(1)}, u32[]{:S(2)}, u32[]{:S(2)}) %all-to-all-start.2) | async-done | bytes 131104 | tf_op jit(solution)/shard_map/all_to_all | solution.py:92
  77.9 4.3 %scatter_custom_fusion = f32[6144,256]{1,0:T(8,128)} fusion(s32[128]{0:T(128)S(1)} %fusion.57, f32[]{:T(128)} %constant.10.clone.1, f32[16,8,256]{2,1,0:T(8,128)S(1)} %all-to-all-done.2), kind=kCustom, calls=%fused_computation.10 | custom fusion | flops 32768 | bytes 6422532 | tf_op jit(solution)/shard_map/scatter-add | solution.py:102
  82.2 111.1 %all-reduce.2.cloned.1.call-done = f32[8,256,256]{2,1,0:T(8,128)} async-done(((f32[8,256,256]{2,1,0:T(8,128)}), f32[8,256,256]{2,1,0:T(8,128)}) %all-reduce.2.cloned.1.call-update) | async-done | bytes 2097168 | tf_op jit(solution)/shard_map/psum | solution.py:86
  193.3 3.1 %broadcast_multiply_fusion = f32[8,256,256]{2,1,0:T(8,128)} fusion(f32[8,256,256]{2,1,0:T(8,128)} %all-reduce.2.cloned.1.call-done), kind=kLoop, calls=%fused_computation.39 | loop fusion | flops 524288 | bytes 4194304 | tf_op jit(solution)/shard_map/mul | solution.py:89
  196.4 3.2 %convert_element_type.103 = bf16[3072,256]{1,0:T(8,128)(2,1)} convert(f32[3072,256]{1,0:T(8,128)} %reduce-scatter.2.cloned.1.call-done) | non-fusion elementwise | flops 786432 | bytes 4718592 | tf_op jit(solution)/shard_map/convert_element_type | solution.py:105
  (41 shorter events, 6.3 us)
Async XLA Ops:
  8.0 17.4 %copy-start = (bf16[6144,256]{1,0:T(8,128)(2,1)S(1)}, bf16[6144,256]{1,0:T(8,128)(2,1)}, u32[]{:S(2)}) copy-start(bf16[6144,256]{1,0:T(8,128)(2,1)} %param.8) | copy-start | bytes 9437188
  9.5 15.5 %all-to-all-start = ((s32[16,1,8]{2,1,0:T(1,128)}), s32[16,1,8]{2,1,0:T(1,128)S(1)}, u32[]{:S(2)}, u32[]{:S(2)}) async-start(s32[16,1,8]{2,1,0:T(1,128)} %copy.21), calls=%async_computation | async-start | bytes 16384 | tf_op jit(solution)/shard_map/all_to_all | solution.py:45
  27.0 12.0 %all-to-all-start.1 = ((bf16[16,8,256]{2,1,0:T(8,128)(2,1)}), bf16[16,8,256]{2,1,0:T(8,128)(2,1)S(1)}, u32[]{:S(2)}, u32[]{:S(2)}) async-start(bf16[16,8,256]{2,1,0:T(8,128)(2,1)} %bitcast_select_fusion), calls=%async_computation.1 | async-start | bytes 131072 | tf_op jit(solution)/shard_map/all_to_all | solution.py:47
  31.4 161.9 %all-reduce.2.cloned.1.call-start = ((), (), s32[]{:S(2)}) async-start(), calls=%async_computation.5 | async-start | bytes 4194304 | tf_op jit(solution)/shard_map/psum | solution.py:86
  41.9 1.3 copy-start.3
  43.2 2.0 copy-start.4
  59.5 2.6 %copy-start.1 = (f32[1024,256]{1,0:T(8,128)S(1)}, f32[1024,256]{1,0:T(8,128)}, u32[]{:S(2)}) copy-start(f32[1024,256]{1,0:T(8,128)} %fusion.48) | copy-start | bytes 3145732
  59.5 2.6 %copy-start.2 = (f32[1024,256]{1,0:T(8,128)S(1)}, f32[1024,256]{1,0:T(8,128)}, u32[]{:S(2)}) copy-start(f32[1024,256]{1,0:T(8,128)} %convert_multiply_fusion.2) | copy-start | bytes 3145732
  64.9 13.0 %all-to-all-start.2 = ((f32[16,8,256]{2,1,0:T(8,128)}), f32[16,8,256]{2,1,0:T(8,128)S(1)}, u32[]{:S(2)}, u32[]{:S(2)}) async-start(f32[16,8,256]{2,1,0:T(8,128)} %fusion.23), calls=%async_computation.2 | async-start | bytes 262144 | tf_op jit(solution)/shard_map/all_to_all | solution.py:92
  69.7 126.7 %reduce-scatter.2.cloned.1.call-start = ((), (), s32[]{:S(2)}) async-start(), calls=%async_computation.4 | async-start | bytes 9437184 | tf_op jit(solution)/shard_map/reduce_scatter | solution.py:104
Sparse Core Ops, SparseCore 0:
  59.6 133.6 all-reduce.1
Sparse Core Ops, SparseCore 1:
  82.3 12.0 reduce-scatter.1
where the time goes:
time: 208 us; the launch traced here: 207 us
  waiting for transfers between devices  123 us (59%)
  matrix products  22.5 us (11%)
  between operations  19.8 us (10%)
  other arithmetic  19 us (9%)
  starting transfers between devices  17.6 us (8%)
  local copies, waits for them, and re-layouts  5.52 us (3%)
    psum x1, waiting for transfers between devices, shards(): operator_total = lax.psum(operator_acc, ('rows', 'rep'))  111 us
    all_to_all x1, starting transfers between devices, shards(): lax.all_to_all(requests, 'rows', split_axis=0, concat_axis=0, tiled=True)  8.31 us
    all_to_all x1, waiting for transfers between devices, shards(): lax.all_to_all(slot_grad.reshape(owner_count, capacity, row_width), 'rows...  6.83 us
    all_to_all x1, starting transfers between devices, shards(): lax.all_to_all(slot_grad.reshape(owner_count, capacity, row_width), 'rows...  4.82 us
    all_to_all x1, starting transfers between devices, shards(): lax.all_to_all(serve_picked, 'rows', split_axis=0, concat_axis=0, tiled=T...  4.43 us
    scatter-add x1, other arithmetic, shards(): jnp.zeros((entity_table.shape[0], row_width), jnp.float32).at[flat_index]  4.29 us
  transfers between devices with their start and end apart: 5, of which 4 were waited for; matrix products, arithmetic and copies ran while one was open for 10% of the time, Pallas kernels for 0%

commit v1 on v0

--- a/solution.py
+++ b/solution.py
@@ -83,7 +83,7 @@
         )
         chosen = (relation_lane == relations[block_index]).astype(jnp.float32)
         operator_acc = operator_acc + chosen[:, None, None] * operator_grad[None, :, :]
-    operator_total = lax.psum(operator_acc, ("rows", "rep"))
+    operator_total = lax.psum(lax.psum(operator_acc, "rep"), "rows")
     devices = lax.axis_size("rows") * lax.axis_size("rep")
     relation_grad = (
         operator_total

time: 208 us -> 236 us (1.13)
  waiting for transfers between devices: 123 us -> 145 us
  matrix products: 22.5 us -> 25 us
    reduce_scatter x1, waiting for transfers between devices: 0.01 us -> 13.1 us  [shards(): lax.psum_scatter(owner_slab, 'rep', scatter_dimension=0, tiled=True)]
    psum x1 -> x2, waiting for transfers between devices: 111 us -> 118 us  [shards(): operator_total = lax.psum(lax.psum(operator_acc, 'rep'), 'rows')]
    dot_general x2, matrix products: 2.8 us -> 5.4 us  [shards(): jnp.einsum('rs,rd->sd', picker, upper_part, preferred_element_type=jnp.fl...]
  transfers between devices with their start and end apart: 5 -> 6, of which waited for: 4 -> 6; matrix products, arithmetic and copies ran while one was open for 10% -> 13% of each run, Pallas kernels for 0% -> 0%
where the time goes in v1:
time: 236 us; the launch traced here: 235 us
  waiting for transfers between devices  145 us (61%)
  matrix products  25 us (11%)
  starting transfers between devices  19.8 us (8%)
  other arithmetic  19.8 us (8%)
  between operations  18.1 us (8%)
  local copies, waits for them, and re-layouts  7.76 us (3%)
    psum x2, waiting for transfers between devices, shards(): operator_total = lax.psum(lax.psum(operator_acc, 'rep'), 'rows')  118 us
    reduce_scatter x1, waiting for transfers between devices, shards(): lax.psum_scatter(owner_slab, 'rep', scatter_dimension=0, tiled=True)  13.1 us
    all_to_all x1, waiting for transfers between devices, shards(): lax.all_to_all(slot_grad.reshape(owner_count, capacity, row_width), 'rows...  9.17 us
    all_to_all x1, starting transfers between devices, shards(): lax.all_to_all(requests, 'rows', split_axis=0, concat_axis=0, tiled=True)  8.31 us
    all_to_all x1, starting transfers between devices, shards(): lax.all_to_all(slot_grad.reshape(owner_count, capacity, row_width), 'rows...  6.79 us
    dot_general x2, matrix products, shards(): jnp.einsum('rs,rd->sd', picker, upper_part, preferred_element_type=jnp.fl...  5.4 us
  transfers between devices with their start and end apart: 6, of which 6 were waited for; matrix products, arithmetic and copies ran while one was open for 13% of the time, Pallas kernels for 0%

profile of v1, /device:TPU:0, one launch (start us, length us, event | category | flops | bytes accessed | tf_op | source)
XLA Modules:
  0.0 235.4 jit_solution(14973035856496258693)
XLA Ops:
  7.2 1.5 copy.21
  8.7 8.3 %all-to-all-start = ((s32[16,1,8]{2,1,0:T(1,128)}), s32[16,1,8]{2,1,0:T(1,128)S(1)}, u32[]{:S(2)}, u32[]{:S(2)}) async-start(s32[16,1,8]{2,1,0:T(1,128)} %copy.21), calls=%async_computation | async-start | bytes 16384 | tf_op jit(solution)/shard_map/all_to_all | solution.py:45
  17.8 1.0 convert_reduce_fusion
  20.3 1.4 fusion.69
  21.7 2.5 %all-to-all-done = s32[16,1,8]{2,1,0:T(1,128)S(1)} async-done(((s32[16,1,8]{2,1,0:T(1,128)}), s32[16,1,8]{2,1,0:T(1,128)S(1)}, u32[]{:S(2)}, u32[]{:S(2)}) %all-to-all-start) | async-done | bytes 544 | tf_op jit(solution)/shard_map/all_to_all | solution.py:45
  24.6 0.8 gather_fusion
  26.1 4.4 %all-to-all-start.1 = ((bf16[16,8,256]{2,1,0:T(8,128)(2,1)}), bf16[16,8,256]{2,1,0:T(8,128)(2,1)S(1)}, u32[]{:S(2)}, u32[]{:S(2)}) async-start(bf16[16,8,256]{2,1,0:T(8,128)(2,1)} %bitcast_select_fusion), calls=%async_computation.1 | async-start | bytes 131072 | tf_op jit(solution)/shard_map/all_to_all | solution.py:47
  30.6 1.3 compare_convert_fusion
  36.0 2.1 all-to-all-done.1
  38.1 1.6 convolution_convert_fusion
  39.7 1.3 fusion.27
  41.1 1.6 convolution_convert_fusion.1
  42.7 1.3 fusion.26
  44.0 1.3 multiply_convert_fusion.1
  47.5 1.3 multiply_convert_fusion
  51.0 1.6 multiply_add_fusion
  52.8 2.2 convert_multiply_fusion
  55.1 3.4 %fusion.71 = f32[1024,256]{1,0:T(8,128)} fusion(bf16[1024,1024]{1,0:T(8,128)(2,1)} %copy-done.10, bf16[1024,256]{1,0:T(8,128)(2,1)} %copy-done.4), kind=kOutput, calls=%fused_computation.106 | convolution fusion | flops 536870912 | bytes 3670016 | tf_op jit(solution)/shard_map/bn,bd->nd/dot_general | solution.py:26
  58.4 14.8 %all-reduce.3.cloned.1.call-done = f32[8,256,256]{2,1,0:T(8,128)} async-done(((f32[8,256,256]{2,1,0:T(8,128)}), f32[8,256,256]{2,1,0:T(8,128)}) %all-reduce.3.cloned.1.call-update) | async-done | bytes 2097168 | tf_op jit(solution)/shard_map/psum | solution.py:86
  73.2 1.4 fusion.45
  74.6 3.6 %fusion.5 = f32[128,256]{1,0:T(8,128)S(1)} fusion(f32[1024,256]{1,0:T(8,128)} %fusion.71, f32[1024,256]{1,0:T(8,128)} %convert_multiply_fusion, f32[1024,256]{1,0:T(8,128)S(1)} %fusion.45, s32[3072]{0:T(1024)S(1)} %pad_add_fusion.1), kind=kOutput, calls=%fused_computation.17 | convolution fusion | flops 206438400 | bytes 3289088 | tf_op jit(solution)/shard_map/rs,rd->sd/dot_general | solution.py:78
  78.3 1.1 fusion.4
  79.4 1.4 fusion.48
  81.9 1.1 fusion.6
  82.9 1.8 fusion.23
  84.7 6.8 %all-to-all-start.2 = ((f32[16,8,256]{2,1,0:T(8,128)}), f32[16,8,256]{2,1,0:T(8,128)S(1)}, u32[]{:S(2)}, u32[]{:S(2)}) async-start(f32[16,8,256]{2,1,0:T(8,128)} %fusion.23), calls=%async_computation.2 | async-start | bytes 262144 | tf_op jit(solution)/shard_map/all_to_all | solution.py:92
  92.8 9.2 %all-to-all-done.2 = f32[16,8,256]{2,1,0:T(8,128)S(1)} async-done(((f32[16,8,256]{2,1,0:T(8,128)}), f32[16,8,256]{2,1,0:T(8,128)S(1)}, u32[]{:S(2)}, u32[]{:S(2)}) %all-to-all-start.2) | async-done | bytes 131104 | tf_op jit(solution)/shard_map/all_to_all | solution.py:92
  102.0 4.3 %scatter_custom_fusion = f32[6144,256]{1,0:T(8,128)} fusion(s32[128]{0:T(128)S(1)} %fusion.57, f32[]{:T(128)} %constant.10.clone.1, f32[16,8,256]{2,1,0:T(8,128)S(1)} %all-to-all-done.2), kind=kCustom, calls=%fused_computation.10 | custom fusion | flops 32768 | bytes 6422532 | tf_op jit(solution)/shard_map/scatter-add | solution.py:102
  106.3 103.1 %all-reduce.5.cloned.1.call-done = f32[8,256,256]{2,1,0:T(8,128)} async-done(((f32[8,256,256]{2,1,0:T(8,128)}), f32[8,256,256]{2,1,0:T(8,128)}) %all-reduce.5.cloned.1.call-update) | async-done | bytes 2097168 | tf_op jit(solution)/shard_map/psum | solution.py:86
  209.5 3.1 %broadcast_multiply_fusion = f32[8,256,256]{2,1,0:T(8,128)} fusion(f32[8,256,256]{2,1,0:T(8,128)} %all-reduce.5.cloned.1.call-done), kind=kLoop, calls=%fused_computation.39 | loop fusion | flops 524288 | bytes 4194304 | tf_op jit(solution)/shard_map/mul | solution.py:89
  212.6 13.1 %reduce-scatter.2.cloned.1.call-done = f32[3072,256]{1,0:T(8,128)} async-done(((f32[6144,256]{1,0:T(8,128)}), f32[3072,256]{1,0:T(8,128)}) %reduce-scatter.2.cloned.1.call-update) | async-done | bytes 3145744 | tf_op jit(solution)/shard_map/reduce_scatter | solution.py:104
  225.7 3.2 %convert_element_type.103 = bf16[3072,256]{1,0:T(8,128)(2,1)} convert(f32[3072,256]{1,0:T(8,128)} %reduce-scatter.2.cloned.1.call-done) | non-fusion elementwise | flops 786432 | bytes 4718592 | tf_op jit(solution)/shard_map/convert_element_type | solution.py:105
  (58 shorter events, 10.3 us)
Async XLA Ops:
  7.2 17.4 %copy-start = (bf16[6144,256]{1,0:T(8,128)(2,1)S(1)}, bf16[6144,256]{1,0:T(8,128)(2,1)}, u32[]{:S(2)}) copy-start(bf16[6144,256]{1,0:T(8,128)(2,1)} %param.8) | copy-start | bytes 9437188
  8.7 15.5 %all-to-all-start = ((s32[16,1,8]{2,1,0:T(1,128)}), s32[16,1,8]{2,1,0:T(1,128)S(1)}, u32[]{:S(2)}, u32[]{:S(2)}) async-start(s32[16,1,8]{2,1,0:T(1,128)} %copy.21), calls=%async_computation | async-start | bytes 16384 | tf_op jit(solution)/shard_map/all_to_all | solution.py:45
  26.1 12.0 %all-to-all-start.1 = ((bf16[16,8,256]{2,1,0:T(8,128)(2,1)}), bf16[16,8,256]{2,1,0:T(8,128)(2,1)S(1)}, u32[]{:S(2)}, u32[]{:S(2)}) async-start(bf16[16,8,256]{2,1,0:T(8,128)(2,1)} %bitcast_select_fusion), calls=%async_computation.1 | async-start | bytes 131072 | tf_op jit(solution)/shard_map/all_to_all | solution.py:47
  30.6 42.6 %all-reduce.3.cloned.1.call-start = ((), (), s32[]{:S(2)}) async-start(), calls=%async_computation.5 | async-start | bytes 4194304 | tf_op jit(solution)/shard_map/psum | solution.py:86
  41.0 6.5 %copy-start.4 = (bf16[1024,256]{1,0:T(8,128)(2,1)}, bf16[1024,256]{1,0:T(8,128)(2,1)S(1)}, u32[]{:S(2)}) copy-start(bf16[1024,256]{1,0:T(8,128)(2,1)S(1)} %get-tuple-element.23) | copy-start | bytes 1572868
  44.0 1.3 copy-start.2
  45.4 1.4 copy-start.8
  46.7 0.8 copy-start.5
  48.8 1.3 copy-start.10
  50.2 0.8 copy-start.7
  52.6 156.9 %all-reduce.5.cloned.1.call-start = ((), (), s32[]{:S(2)}) async-start(), calls=%async_computation.6 | async-start | bytes 4194304 | tf_op jit(solution)/shard_map/psum | solution.py:86
  74.6 3.7 %copy-start.1 = (f32[1024,256]{1,0:T(8,128)S(1)}, f32[1024,256]{1,0:T(8,128)}, u32[]{:S(2)}) copy-start(f32[1024,256]{1,0:T(8,128)} %convert_multiply_fusion) | copy-start | bytes 3145732
  74.6 3.7 %copy-start.11 = (f32[1024,256]{1,0:T(8,128)S(1)}, f32[1024,256]{1,0:T(8,128)}, u32[]{:S(2)}) copy-start(f32[1024,256]{1,0:T(8,128)} %fusion.71) | copy-start | bytes 3145732
  78.3 1.1 copy-start.6
  78.3 2.5 %copy-start.3 = (bf16[1024,256]{1,0:T(8,128)(2,1)S(1)}, bf16[1024,256]{1,0:T(8,128)(2,1)}, u32[]{:S(2)}) copy-start(bf16[1024,256]{1,0:T(8,128)(2,1)} %copy-done.2) | copy-start | bytes 1572868
  79.4 1.7 copy-start.9
  84.7 17.3 %all-to-all-start.2 = ((f32[16,8,256]{2,1,0:T(8,128)}), f32[16,8,256]{2,1,0:T(8,128)S(1)}, u32[]{:S(2)}, u32[]{:S(2)}) async-start(f32[16,8,256]{2,1,0:T(8,128)} %fusion.23), calls=%async_computation.2 | async-start | bytes 262144 | tf_op jit(solution)/shard_map/all_to_all | solution.py:92
  91.5 134.1 %reduce-scatter.2.cloned.1.call-start = ((), (), s32[]{:S(2)}) async-start(), calls=%async_computation.4 | async-start | bytes 9437184 | tf_op jit(solution)/shard_map/reduce_scatter | solution.py:104
Sparse Core Ops, SparseCore 0:
  52.7 20.4 all-reduce.2
  79.6 129.8 all-reduce.4
  211.8 13.8 reduce-scatter.1
